TPU v7x, 32 devices: a whole 2x2x4 slice. The times are simulated.
32 devices in a mesh: dp: 4 (over y, x), ctx: 4 (over z), tensor: 2 (over core).
Axes of the slice: x: 2, y: 2, z: 4, core: 2. Of those that a mesh axis runs over, the one named last changes fastest.
Arguments:
- seq_in: bfloat16 [4, 2048, 5120], P('dp', 'ctx', 'tensor'), may hold values from -6 to 6
- gate_in: bfloat16 [4, 2048, 5120], P('dp', 'ctx', 'tensor'), may hold values from -96 to 96
- keys_in: bfloat16 [4, 2048, 128], P('dp', 'ctx'), may hold values from -0.5 to 0.5
- queries_in: bfloat16 [4, 2048, 128], P('dp', 'ctx'), may hold values from -0.5 to 0.5
- step_rate: float32 [4, 2048, 80], P('dp', 'ctx', 'tensor'), may hold values from 0 to 1, as said below
- doc_starts: int32 [4, 4], P('dp', 'ctx'), may hold values from 0 to 512, as said below
- skip_gain: float32 [80], P('tensor'), may hold values from 0.5 to 1.5
- norm_gain: float32 [5120], P('tensor'), may hold values from 0.5 to 1.5
- prompt_in: bfloat16 [32, 5120], P(None, 'tensor'), may hold values from -6 to 6
- prompt_keys: bfloat16 [32, 128], replicated, may hold values from -0.5 to 0.5
- prompt_rate: float32 [32, 80], P(None, 'tensor'), may hold values from 0.01 to 0.1
- start_state: float32 [128, 5120], P(None, 'tensor'), may hold values from -6 to 6
- out_grad: bfloat16 [4, 2048, 5120], P('dp', 'ctx', 'tensor'), may hold values from -6 to 6
Outputs:
- normed: bfloat16 [4, 2048, 5120], P('dp', 'ctx', 'tensor')
- grad_in: bfloat16 [4, 2048, 5120], P('dp', 'ctx', 'tensor')
- grad_gate: bfloat16 [4, 2048, 5120], P('dp', 'ctx', 'tensor')
- grad_prompt: float32 [32, 5120], P(None, 'tensor')
- grad_start: float32 [128, 5120], P(None, 'tensor')
Inputs may be any that keep to these rules, and one draw needn't show every extreme that they name: doc_starts[b, c] is the position within block c of sequence b at which a new document begins, 512 where none begins in that block; at most one begins in a block. `step_rate`: Positive.
All inputs are finite; a program needn't handle non-finite values.
Results may differ from a plain program's by a relative error of at most 0.006.
Values sent between devices are 32-bit elements; how exact they have to be, the bound alone decides.
No kernel may reach another device: no remote copies, remote signals or barrier semaphores. Data moves between devices by JAX's collectives and lax.ppermute only.
A program may use at most 256 MiB of HBM per device.

v0:
```python
import functools

import jax
import jax.numpy as jnp
from jax import lax
from jax.experimental import pallas as pl
from jax.experimental.pallas import tpu as pltpu
from jax.sharding import PartitionSpec as P

HEAD_DIM = 64
EPSILON = 1e-05
LANES = 128
VLIM = 32
BETWEEN = 4
WAITED = 3
LATE = 4
PLIM = 24
GROUP = 8
KIND_IN, KIND_OUT = 1, 3
EXTRA = 8
ROWS = 128

F32 = jnp.float32
BF16 = jnp.bfloat16
EXACT = lax.Precision.HIGHEST


def iota(shape, dim):
    return lax.broadcasted_iota(jnp.int32, shape, dim)


def mm(a, b, da=1, db=0, precision=None):
    return lax.dot_general(
        a, b, (((da,), (db,)), ((), ())), precision=precision, preferred_element_type=F32
    )


def two_heads(table, first):
    rows = table.shape[0]
    left = jnp.broadcast_to(table[:, first : first + 1], (rows, LANES))
    right = jnp.broadcast_to(table[:, first + 1 : first + 2], (rows, LANES))
    return jnp.where(iota((rows, LANES), 1) < HEAD_DIM, left, right)


def spread_weights(wide, kind, width):
    lane, col = iota((LANES, width), 0), iota((LANES, width), 1)
    part = lane // GROUP
    hit = ((part == kind) | (part == kind + 1)) & ((lane & (GROUP - 1)) == col // HEAD_DIM)
    return mm(wide, jnp.where(hit, 1.0, 0.0).astype(BF16))


def split_queries(queries, doc_start):
    rows, width = queries.shape
    ahead = iota((rows, width), 0) < doc_start
    wide = queries.astype(F32)
    both = [jnp.where(ahead, wide, 0.0), jnp.where(ahead, 0.0, wide)]
    return jnp.concatenate(both, axis=1).astype(BF16)


def tile(p):
    return slice(p * LANES, (p + 1) * LANES)


def row_block(i):
    return slice(i * ROWS, (i + 1) * ROWS)


def each_pair(one):
    def step(p, carry):
        one(p, pl.ds(pl.multiple_of(p * LANES, LANES), LANES))
        return carry

    lax.fori_loop(0, GROUP // 2, step, 0)


def each_block(rows, one):
    def step(i, carry):
        one(pl.ds(pl.multiple_of(i * ROWS, ROWS), ROWS))
        return carry

    lax.fori_loop(0, rows // ROWS, step, 0)


def turn(table, p):
    return pltpu.roll(table, lax.rem(LANES - 2 * p, LANES), 1)


def call(kernel, outs, ins, out_shapes, scratch=(), alias=None, limit=16, steps=1):
    return pl.pallas_call(
        kernel,
        grid=(steps,),
        in_specs=ins,
        out_specs=outs,
        out_shape=out_shapes,
        scratch_shapes=list(scratch),
        input_output_aliases=alias or {},
        cost_estimate=pl.CostEstimate(flops=0, bytes_accessed=0, transcendentals=0),
        compiler_params=pltpu.CompilerParams(vmem_limit_bytes=limit * 2**20),
    )


def whole(array):
    zeros = (0,) * array.ndim
    return pl.BlockSpec(array.shape, lambda s: zeros)


def columns(array, k, width):
    lead = (0,) * (array.ndim - 1)
    return pl.BlockSpec(array.shape[:-1] + (width,), lambda s: lead + (k,))


SCALAR = pl.BlockSpec(memory_space=pltpu.SMEM)
ANYWHERE = pl.BlockSpec(memory_space=pl.ANY)


def silu(value):
    sigmoid = 0.5 + 0.5 * jnp.tanh(0.5 * value)
    return value * sigmoid, sigmoid


def open_kernel(
    k, doc, step_ref, keys, seq, prompt_in, prompt_keys, rate, state,
    tab_ref, wide_ref, first_ref, move_ref, late_ref, mine_ref, through_ref, low_ref, cols_ref,
):
    heads, rows = step_ref.shape[1:]
    doc_start = doc[0, 0]
    step = step_ref[0]
    hh, ll = iota((heads, LANES), 0), iota((heads, LANES), 1)
    spread = jnp.where((ll < 5 * GROUP) & (hh == k * GROUP + (ll & (GROUP - 1))), 1.0, 0.0)
    spread = spread.astype(BF16)
    tri = jnp.where(iota((rows, rows), 0) >= iota((rows, rows), 1), 1.0, 0.0).astype(BF16)
    high = step.astype(BF16)
    rest = step - high.astype(F32)
    middle = rest.astype(BF16)
    low = (rest - middle.astype(F32)).astype(BF16)
    step_rep = jnp.zeros((rows, LANES), F32)
    cum = jnp.zeros((rows, LANES), F32)
    for part in (low, middle, high):
        rep = mm(part, spread, 0, 0)
        step_rep = step_rep + rep
        cum = cum + mm(tri, rep.astype(BF16))
    before = cum - step_rep
    pos = iota((rows, LANES), 0)
    kind = iota((rows, LANES), 1) // GROUP
    has = doc_start < rows
    ex_start = jnp.sum(jnp.where(pos == doc_start, before, 0.0), axis=0, keepdims=True)
    end = cum[rows - 1 : rows]
    tail_start = jnp.where(has, doc_start, 0)
    arg = jnp.where(kind < KIND_OUT, jnp.where(pos < doc_start, 0.0, ex_start) - cum, cum - end)
    keep = (kind < KIND_OUT) | (pos >= tail_start)
    weights = jnp.where(keep, jnp.exp(jnp.minimum(arg, 0.0)), 0.0)
    tab_ref[...] = cum
    head_part = weights.astype(BF16).astype(F32)
    is_head = (kind == KIND_IN) | (kind == KIND_OUT)
    wide = jnp.where(is_head, head_part, weights - head_part).astype(BF16)
    wide_ref[...] = wide
    through = jnp.where(has, 0.0, jnp.exp(-end))
    leave = jnp.where(has, jnp.exp(ex_start - end), 0.0)

    prompt_rows = rate.shape[0]
    square = (prompt_rows, prompt_rows)
    later = jnp.where(iota(square, 0) < iota(square, 1), 1.0, 0.0)
    spread_weight = jnp.exp(-mm(later, rate[...], precision=EXACT))
    carry = jnp.exp(-jnp.sum(rate[...], axis=0, keepdims=True))
    for p in range(GROUP // 2):
        cols_ref[:prompt_rows, tile(p)] = two_heads(spread_weight, k * GROUP + 2 * p)
        for place, row in ((0, two_heads(carry, k * GROUP + 2 * p)), (8, two_heads(through, 2 * p))):
            rows_here = slice(prompt_rows + place, prompt_rows + place + 8)
            cols_ref[rows_here, tile(p)] = jnp.broadcast_to(row, (8, LANES))
        cols_ref[prompt_rows + 16 : prompt_rows + 24, tile(p)] = jnp.broadcast_to(
            two_heads(leave, 2 * p), (8, LANES)
        )
    state_rows, width = state.shape
    weighted = (seq[0].astype(F32) * spread_weights(wide, KIND_OUT, width)).astype(BF16)
    field = mm(
        prompt_keys[...].astype(F32), cols_ref[:prompt_rows] * prompt_in[...].astype(F32), 0, 0, EXACT
    )
    start = field + cols_ref[prompt_rows : prompt_rows + 1] * state[...]
    through_cols = cols_ref[prompt_rows + 8 : prompt_rows + 9]
    through_ref[...] = jnp.broadcast_to(through_cols, through_ref.shape)
    leave_cols = cols_ref[prompt_rows + 16 : prompt_rows + 17]
    move = mm(keys[0], weighted, 0, 0) + leave_cols * start
    is_first = lax.axis_index("ctx") == 0
    low_ref[...] = start.astype(BF16)
    mine_ref[:state_rows] = jnp.where(is_first, start, 0.0)
    move_ref[:state_rows] = move
    late_ref[:state_rows] = move
    first_ref[:state_rows] = through_cols * start + move
    ones = jnp.ones((EXTRA, width), F32)
    mine_ref[state_rows:] = jnp.where(is_first, ones, 0.0)
    extra = jnp.broadcast_to(leave_cols, (EXTRA, width))
    move_ref[state_rows:] = extra
    late_ref[state_rows:] = extra
    first_ref[state_rows:] = through_cols + extra


def open_from_hbm(ks, cut, outs, doc, *refs):
    ins = len(cut)
    held, buffers, sems = refs[:ins], refs[-1 - ins : -1], refs[-1]
    made = refs[-1 - ins - outs * len(ks) : -1 - ins]
    copies = []
    for n, (source, buffer) in enumerate(zip(held, buffers)):
        width = buffer.shape[-1]
        columns_here = pl.ds(ks[0] * (width // len(ks)) if cut[n] else 0, width)
        lead = (slice(None),) * (len(buffer.shape) - 1)
        copies.append(pltpu.make_async_copy(source.at[lead + (columns_here,)], buffer, sems.at[n]))
    for copy in copies:
        copy.start()
    for copy in copies:
        copy.wait()
    for place, k in enumerate(ks):
        mine = []
        for buffer, is_cut in zip(buffers, cut):
            width = buffer.shape[-1] // len(ks)
            lead = (slice(None),) * (len(buffer.shape) - 1)
            mine.append(buffer.at[lead + (pl.ds(place * width, width),)] if is_cut else buffer)
        open_kernel(k, doc, *mine, *made[place * outs : (place + 1) * outs])


def step_kernel(arrived, move, through, *rest):
    mine, (sum_ref, send_ref) = rest[:-2], rest[-2:]
    total = arrived[...] if not mine else mine[0][...] + arrived[...]
    sum_ref[...] = total
    send_ref[...] = through[: total.shape[0]] * total + move[...]


def head_halves():
    lane = iota((1, LANES), 1)
    return [jnp.where(half, 1.0, 0.0).astype(BF16) for half in (lane < HEAD_DIM, lane >= HEAD_DIM)]


def within_kernel(k, doc, tab_ref, keys, queries, seq, skip, base_ref, cum_rows, scores, skips):
    rows = tab_ref.shape[0]
    doc_start = doc[0, 0]
    halves = head_halves()
    turned_sums = jnp.transpose(tab_ref[...])
    for h in range(GROUP):
        cum_rows[h] = jnp.broadcast_to(turned_sums[h : h + 1], cum_rows.shape[1:])
    for p in range(GROUP // 2):
        skips[:, tile(p)] = jnp.broadcast_to(two_heads(skip[...], k * GROUP + 2 * p), (8, LANES))
    for i in range(rows // ROWS):
        upto = (i + 1) * ROWS
        t = iota((ROWS, upto), 0) + i * ROWS
        s = iota((ROWS, upto), 1)
        same = (s <= t) & ((t < doc_start) | (s >= doc_start))
        scores[row_block(i), :upto] = jnp.where(same, mm(queries[0, row_block(i)], keys[0, :upto], 1, 1), 0.0)

    def pair(p, here):
        turned = turn(tab_ref[...], p)
        values = [seq[0, :, here] * half for half in halves]
        for i in range(rows // ROWS):
            upto = (i + 1) * ROWS
            total = skips[:1, here] * seq[0, row_block(i), here].astype(F32)
            for half in range(2):
                gap = cum_rows[2 * p + half, :1, :upto] - turned[row_block(i), half : half + 1]
                mixing = (scores[row_block(i), :upto] * jnp.exp(jnp.minimum(gap, 0.0))).astype(BF16)
                total += mm(mixing, values[half][:upto])
            base_ref[row_block(i), here] = total

    each_pair(pair)


def gate_kernel(
    doc, wide, base, mine, arrived, low, queries, gate, grad, gain, before, *rest
):
    out_ref, stat_ref, share_ref = rest[-3:]
    rows, width = base.shape
    state_rows = low.shape[0]
    state_in = mine[...] + arrived[...]
    share_ref[...] = state_in[state_rows:]
    fields = jnp.concatenate([state_in[:state_rows].astype(BF16), low[...]], axis=0)
    reads = mm(split_queries(queries[0], doc[0, 0]), fields)
    weights = spread_weights(wide[...], KIND_IN, width)
    for i in range(rows // ROWS):
        rb = row_block(i)
        squares = jnp.zeros((ROWS, LANES), F32)
        inner = jnp.zeros((ROWS, LANES), F32)
        for p in range(GROUP // 2):
            out = (base[rb, tile(p)] + weights[rb, tile(p)] * reads[rb, tile(p)]).astype(BF16)
            out_ref[rb, tile(p)] = out
            act, _ = silu(gate[0, rb, tile(p)].astype(F32))
            gated = out.astype(F32) * act
            squares += gated * gated
            inner += grad[0, rb, tile(p)].astype(F32) * gain[:, tile(p)] * gated
        lane = iota((ROWS, 8), 1)
        sums = jnp.where(
            lane == 0,
            jnp.sum(squares, axis=1, keepdims=True),
            jnp.where(lane == 1, jnp.sum(inner, axis=1, keepdims=True), 0.0),
        )
        stat_ref[rb] = sums if before is None else before[rb] + sums


def norm_factors(inner_cols, stat):
    inverse = lax.rsqrt(stat[:, 0:1] / inner_cols + EPSILON)
    pull = stat[:, 1:2] * inverse * inverse * inverse / inner_cols
    shape = (stat.shape[0], LANES)
    return jnp.broadcast_to(inverse, shape), jnp.broadcast_to(pull, shape)


def visit_kernel(
    inner_cols, chunks, doc, stat_a, stat_b, out, gate, grad, gain, queries, share, *rest
):
    wides, ssd_ref, weighted, part = rest[:chunks], rest[chunks], rest[-2], rest[-1]
    visits, parts = rest[chunks + 1 : 2 * chunks + 1], rest[2 * chunks + 1 : -2]
    wide = wides[0][...]
    for n in range(1, chunks):
        wide = jnp.where(pl.program_id(0) == n, wides[n][...], wide)
    rows, width = out.shape
    state_rows = queries.shape[2]
    weights = spread_weights(wide, KIND_IN, width)
    for i in range(rows // ROWS):
        rb = row_block(i)
        inverse, pull = norm_factors(inner_cols, stat_a[rb] + stat_b[rb])
        for p in range(GROUP // 2):
            act, _ = silu(gate[0, rb, tile(p)].astype(F32))
            gated = out[rb, tile(p)].astype(F32) * act
            scaled = grad[0, rb, tile(p)].astype(F32) * gain[:, tile(p)]
            ssd = ((inverse * scaled - gated * pull) * act).astype(BF16)
            ssd_ref[rb, tile(p)] = ssd
            weighted[rb, tile(p)] = (weights[rb, tile(p)] * ssd.astype(F32)).astype(BF16)
    both = mm(split_queries(queries[0], doc[0, 0]), weighted[...], 0, 0)
    visit = both[:state_rows]
    for n, visit_ref in enumerate(visits):

        @pl.when(pl.program_id(0) == n)
        def _(visit_ref=visit_ref):
            visit_ref[...] = visit

    part[...] = both[state_rows:] + share[:1] * visit
    span = state_rows // len(parts)
    for d, piece in enumerate(parts):
        owner = lax.rem(lax.axis_index("dp") + d, len(parts))
        piece[...] = part[pl.ds(pl.multiple_of(owner * span, span), span)]


def back_kernel(
    k, inner_cols, doc, tab_ref, keys, queries, stat_a, stat_b, out, gate, grad, gain, ssd_grad, skip, *rest
):
    base_ref, normed_ref, gate_grad_ref, cum_rows, scores, skips = rest[-6:]
    rows = tab_ref.shape[0]
    doc_start = doc[0, 0]
    halves = head_halves()
    turned_sums = jnp.transpose(tab_ref[...])
    for h in range(GROUP):
        cum_rows[h] = jnp.broadcast_to(turned_sums[h : h + 1], cum_rows.shape[1:])
    for p in range(GROUP // 2):
        skips[:, tile(p)] = jnp.broadcast_to(two_heads(skip[...], k * GROUP + 2 * p), (8, LANES))
    for i in range(rows // ROWS):
        down = i * ROWS
        s = iota((ROWS, rows - down), 0) + down
        t = iota((ROWS, rows - down), 1) + down
        same = (s <= t) & ((t < doc_start) | (s >= doc_start))
        scores[row_block(i), down:] = jnp.where(same, mm(keys[0, row_block(i)], queries[0, down:], 1, 1), 0.0)

    def pair(p, here):
        turned = turn(tab_ref[...], p)
        grads = [ssd_grad[:, here] * half for half in halves]
        for i in range(rows // ROWS):
            down = i * ROWS
            total = skips[:1, here] * ssd_grad[row_block(i), here].astype(F32)
            for half in range(2):
                gap = turned[row_block(i), half : half + 1] - cum_rows[2 * p + half, :1, down:]
                mixing = (scores[row_block(i), down:] * jnp.exp(jnp.minimum(gap, 0.0))).astype(BF16)
                total += mm(mixing, grads[half][down:])
            base_ref[row_block(i), here] = total

    each_pair(pair)

    def one(rb):
        inverse, pull = norm_factors(inner_cols, stat_a[rb] + stat_b[rb])
        for p in range(GROUP // 2):
            value = gate[0, rb, tile(p)].astype(F32)
            act, sigmoid = silu(value)
            slope = sigmoid * (1.0 + value * (1.0 - sigmoid))
            wide_out = out[rb, tile(p)].astype(F32)
            gated = wide_out * act
            gains = gain[:, tile(p)]
            scaled = grad[0, rb, tile(p)].astype(F32) * gains
            normed_ref[0, rb, tile(p)] = (gated * inverse * gains).astype(BF16)
            gated_grad = inverse * scaled - gated * pull
            gate_grad_ref[0, rb, tile(p)] = (gated_grad * wide_out * slope).astype(BF16)

    each_block(rows, one)


def close_kernel(wide, base, adjoint, arrived, keys, *rest):
    grad_ref = rest[-1]
    total = arrived[...] if adjoint is None else adjoint[...] + arrived[...]
    reads = mm(keys[0], total.astype(BF16))
    weights = spread_weights(wide[...], KIND_OUT, base.shape[1])
    grad_ref[0] = (base[...] + weights * reads).astype(BF16)


def add_kernel(*refs):
    refs[-1][...] = sum((r[...] for r in refs[1:-1]), refs[0][...])


def split_add_kernel(parts, *refs):
    total, pieces = refs[-1], refs[-1 - parts : -1]
    span = total.shape[1]
    for n in range(parts):
        rows = slice(n * span, (n + 1) * span)
        total[n] = sum((r[rows] for r in refs[1 : -1 - parts]), refs[0][rows])
    for d, piece in enumerate(pieces):
        piece[...] = total[lax.rem(lax.axis_index("ctx") + d, parts)]


def join_kernel(parts, *refs):
    out, total = refs[-2:]
    span = total.shape[1]
    for d, piece in enumerate(refs[:parts]):
        total[lax.rem(lax.axis_index("ctx") + parts - d, parts)] = piece[...]
    for n in range(parts):
        out[n * span : (n + 1) * span] = total[n]


def derive_kernel(chunks, pieces, prompt_keys, *rest):
    cols, parts = rest[:chunks], rest[chunks : chunks + pieces]
    prompt_ref, start_ref, total = rest[chunks + pieces :]
    span = parts[0].shape[0]
    for d, piece in enumerate(parts):
        owner = lax.rem(lax.axis_index("dp") + pieces - d, pieces)
        total[pl.ds(pl.multiple_of(owner * span, span), span)] = piece[...]
    prompt_rows = prompt_keys.shape[0]
    keys = prompt_keys[...].astype(F32)
    for k in range(chunks):
        width = cols[k].shape[1]
        span = slice(k * width, (k + 1) * width)
        grads = total[:, span]
        start_ref[:, span] = cols[k][prompt_rows : prompt_rows + 1] * grads
        prompt_ref[:, span] = cols[k][:prompt_rows] * mm(keys, grads, precision=EXACT)


def ring(count, distance):
    return [(i, (i + distance) % count) for i in range(count)]


def shape(*dims, dtype=F32):
    return jax.ShapeDtypeStruct(dims, dtype)


def body(
    seq_in,
    gate_in,
    keys_in,
    queries_in,
    step_rate,
    doc_starts,
    skip_gain,
    norm_gain,
    prompt_in,
    prompt_keys,
    prompt_rate,
    start_state,
    out_grad,
):
    _, rows, cols = seq_in.shape
    state_rows = keys_in.shape[2]
    heads = step_rate.shape[2]
    prompt_rows = prompt_in.shape[0]
    chunks = heads // GROUP
    width = cols // chunks
    tensors = lax.axis_size("tensor")
    inner_cols = cols * tensors
    count = lax.axis_size("ctx")
    step = jnp.swapaxes(step_rate, 1, 2)
    skip = skip_gain.reshape(1, heads)
    gain = norm_gain.reshape(1, cols)
    each = range(chunks)
    message = shape(state_rows + EXTRA, width)
    summary = shape(state_rows, width)
    block = shape(rows, width)
    block_low = shape(rows, width, dtype=BF16)
    full = shape(*seq_in.shape, dtype=BF16)
    part_shape = shape(state_rows, cols)

    def blocked(array, k):
        return columns(array, k, width)

    def run(kernel, out, ins, after=(), hold=(), alias=None, scratch=(), limit=16, steps=1):
        held = len(ins) + len(after)
        made = held + len(hold)

        def ordered(*refs):
            kernel(*refs[: len(ins)], *refs[made : made + len(out)], *refs[made + len(out) + len(hold) :])

        extra = [(a, ANYWHERE) for a in (*after, *hold)]
        out = list(out)
        results = out + [(shape(*h.shape, dtype=h.dtype), ANYWHERE) for h in hold]
        return call(
            ordered,
            [whole(s) if spec is None else spec for s, spec in results],
            [whole(a) if spec is None else spec for a, spec in ins + extra],
            [s for s, _ in results],
            alias={**(alias or {}), **{held + i: len(out) + i for i in range(len(hold))}},
            scratch=scratch,
            limit=limit,
            steps=steps,
        )(*[a for a, _ in ins + extra])

    tabs, wides, firsts, moves, lates, sums, throughs, lows, col_tabs = ([] for _ in range(9))
    made = (tabs, wides, firsts, moves, lates, sums, throughs, lows, col_tabs)
    made_shapes = [
        shape(rows, LANES),
        shape(rows, LANES, dtype=BF16),
        message,
        message,
        message,
        message,
        message,
        shape(state_rows, width, dtype=BF16),
        shape(prompt_rows + 24, width),
    ]

    def open_chunks(ks, after):
        ins = [
            (step, False),
            (keys_in, False),
            (seq_in, True),
            (prompt_in, True),
            (prompt_keys, False),
            (prompt_rate, False),
            (start_state, True),
        ]
        cut = [c for _, c in ins]
        blocks = [a.shape[:-1] + (len(ks) * width,) if c else a.shape for a, c in ins]
        out = run(
            functools.partial(open_from_hbm, ks, cut, len(made)),
            [(s, None) for s in made_shapes] * len(ks),
            [(doc_starts, SCALAR)] + [(a, ANYWHERE) for a, _ in ins],
            after=after,
            scratch=[pltpu.VMEM(b, a.dtype) for b, (a, _) in zip(blocks, ins)]
            + [pltpu.SemaphoreType.DMA((len(ins),))],
            limit=PLIM,
        )
        for place, k in enumerate(ks):
            for held, one in zip(made, out[place * len(made) :]):
                held.append(one)
            arrived[k] = edge_up(firsts[k], 0)

    def chain_step(k, arrived, move, mine, after=()):
        return run(
            step_kernel,
            [(shape(*move.shape), None)] * 2,
            [(arrived, None), (move, None), (throughs[k], None)] + [(m, None) for m in mine],
            after=after,
        )

    def edge_up(array, edge):
        return lax.ppermute(array, "ctx", [(edge, edge + 1)])

    mixing_scratch = [pltpu.VMEM(s, F32) for s in ((GROUP, 8, rows), (rows, rows), (8, width))]

    def within(k, after, hold):
        base, *held = run(
            functools.partial(within_kernel, k),
            [(block, None)],
            [
                (doc_starts, SCALAR),
                (tabs[k], None),
                (keys_in, None),
                (queries_in, None),
                (seq_in, blocked(seq_in, k)),
                (skip, None),
            ],
            after=after,
            hold=hold,
            scratch=mixing_scratch,
        )
        bases.append(base)
        return held

    outs, shares, stats, bases = [], [], [], []
    out_shape, share_shape = shape(rows, cols, dtype=BF16), shape(EXTRA, cols)


    def gates(k, hold):
        kernel, held, alias = gate_kernel, [], {}
        if stats:
            held = [(stats[-1], None), (outs[-1], ANYWHERE), (shares[-1], ANYWHERE)]
            alias = {11: 0, 12: 2}
        else:
            kernel = lambda *refs: gate_kernel(*refs[:10], None, *refs[10:])
        out, stat, share, *held = run(
            kernel,
            [
                (out_shape, blocked(out_shape, k)),
                (shape(rows, 8), None),
                (share_shape, blocked(share_shape, k)),
            ],
            [
                (doc_starts, SCALAR),
                (wides[k], None),
                (bases[k], None),
                (sums[k], None),
                (arrived[k], None),
                (lows[k], None),
                (queries_in, None),
                (gate_in, blocked(gate_in, k)),
                (out_grad, blocked(out_grad, k)),
                (gain, blocked(gain, k)),
            ]
            + held,
            alias=alias,
            hold=hold,
        )
        outs.append(out)
        shares.append(share)
        stats.append(stat)
        return held

    last = count - 2
    arrived = [None] * chunks
    open_chunks([0], [])
    pairs = [list(each)[k : k + 2] for k in range(1, chunks, 2)]
    for ks in pairs[:1]:
        open_chunks(ks, [])
    for edge in range(1, max(last, 2)):
        for k in each:
            sent = []
            if edge < last:
                sums[k], *sent = chain_step(k, arrived[k], moves[k], [sums[k]])
                arrived[k] = edge_up(sent[0], edge)
            if edge == 1 and k + 1 < len(pairs):
                open_chunks(pairs[k + 1], sent)
    lag = 2
    for k in range(chunks + lag):
        if k < chunks:
            if k >= lag:
                gates(k - lag, [])
            sent = []
            if last > 0:
                sums[k], *sent = chain_step(k, arrived[k], lates[k], [sums[k]])
                arrived[k] = edge_up(sent[0], last)
            lates[k + 1 : k + 2] = within(k, sent, lates[k + 1 : k + 2])
        else:
            gates(k - lag, [])
    stat = stats[-1]
    other = lax.ppermute(stat, "tensor", ring(tensors, 1))

    def edge_down(array, edge):
        return lax.ppermute(array, "ctx", [(edge, edge - 1)])

    def edge_down(array, edge):
        return lax.ppermute(array, "ctx", [(edge, edge - 1)])

    def moving(array, width):
        lead = (0,) * (array.ndim - 1)
        return pl.BlockSpec(array.shape[:-1] + (width,), lambda s: lead + (s,))

    groups = lax.axis_size("dp")
    piece = shape(state_rows // groups, cols)
    result = run(
        functools.partial(visit_kernel, inner_cols, chunks),
        [(out_shape, moving(out_shape, width))] + [(summary, None)] * chunks + [(piece, moving(piece, width))] * groups,
        [
            (doc_starts, SCALAR),
            (stat, None),
            (other, None),
            (outs[-1], moving(outs[-1], width)),
            (gate_in, moving(gate_in, width)),
            (out_grad, moving(out_grad, width)),
            (gain, moving(gain, width)),
            (queries_in, None),
            (shares[-1], moving(shares[-1], width)),
        ]
        + [(w, None) for w in wides],
        scratch=[pltpu.VMEM((rows, width), BF16), pltpu.VMEM((state_rows, width), F32)],
        steps=chunks,
        limit=VLIM,
    )
    ssd_grad, visits, parts = result[0], result[1 : 1 + chunks], result[1 + chunks :]
    for k in each:
        arrived[k] = edge_down(visits[k], count - 1)

    back_bases = []
    normed = gate_grad = None

    def back(k, after, hold):
        ins = [
            (doc_starts, SCALAR),
            (tabs[k], None),
            (keys_in, None),
            (queries_in, None),
            (stat, None),
            (other, None),
            (outs[-1], blocked(outs[-1], k)),
            (gate_in, blocked(gate_in, k)),
            (out_grad, blocked(out_grad, k)),
            (gain, blocked(gain, k)),
            (ssd_grad, blocked(ssd_grad, k)),
            (skip, None),
        ]
        alias = {}
        if normed is not None:
            alias = {len(ins): 1, len(ins) + 1: 2}
            ins += [(normed, ANYWHERE), (gate_grad, ANYWHERE)]
        base, *results = run(
            functools.partial(back_kernel, k, inner_cols),
            [(block, None), (full, blocked(full, k)), (full, blocked(full, k))],
            ins,
            after=after,
            hold=hold,
            alias=alias,
            scratch=mixing_scratch,
        )
        back_bases.append(base)
        return results

    normed, gate_grad, *parts = back(0, [], list(parts))
    from_groups = [lax.ppermute(parts[d], "dp", ring(groups, d)) for d in range(1, groups)]
    adjoints = [None] * chunks
    sent = []
    for edge in range(count - 2, 0, -1):
        for k in each:
            held = [] if adjoints[k] is None else [adjoints[k]]
            order = back_bases[-1:] if edge == 1 else []
            adjoints[k], message_out = chain_step(k, arrived[k], visits[k], held, order)
            sent = [message_out]
            arrived[k] = edge_down(message_out, edge)
            if edge == 1 and 0 < k < BETWEEN:
                normed, gate_grad = back(k, sent + [arrived[k - 1]], [])

    small = shape(piece.shape[0] // count, cols)
    mine = run(
        functools.partial(split_add_kernel, count),
        [(small, None)] * count,
        [(p, None) for p in (parts[0], *from_groups)],
        after=sent + back_bases[-1:] + arrived[WAITED : WAITED + 1],
        scratch=[pltpu.VMEM((count,) + small.shape, F32)],
    )
    from_blocks = [lax.ppermute(mine[d], "ctx", ring(count, d)) for d in range(1, count)]
    for k in range(len(back_bases), LATE):
        normed, gate_grad = back(k, [mine[0], arrived[k]], [])
    (own,) = run(add_kernel, [(small, None)], [(p, None) for p in (mine[0], *from_blocks)], after=back_bases[-1:])
    owned = [own] + [lax.ppermute(own, "ctx", ring(count, d)) for d in range(1, count)]
    for k in range(LATE, chunks):
        normed, gate_grad = back(k, [own, arrived[k]], [])
    (total,) = run(
        functools.partial(join_kernel, count),
        [(piece, None)],
        [(p, None) for p in owned],
        after=back_bases[-1:],
        scratch=[pltpu.VMEM((count,) + small.shape, F32)],
    )
    totals = [total] + [lax.ppermute(total, "dp", ring(groups, d)) for d in range(1, groups)]

    grad_in = None
    for k in each:
        ins = [(wides[k], None), (back_bases[k], None)]
        kernel = close_kernel
        if adjoints[k] is None:
            kernel = lambda wide, base, *refs: close_kernel(wide, base, None, *refs)
        else:
            ins.append((adjoints[k], None))
        ins += [(arrived[k], None), (keys_in, None)]
        alias = {}
        if grad_in is not None:
            alias = {len(ins): 0}
            ins.append((grad_in, ANYWHERE))
        (grad_in,) = run(kernel, [(full, blocked(full, k))], ins, alias=alias)

    grad_prompt, grad_start = run(
        functools.partial(derive_kernel, chunks, groups),
        [(shape(prompt_rows, cols), None), (part_shape, None)],
        [(a, None) for a in (prompt_keys, *col_tabs, *totals)],
        scratch=[pltpu.VMEM((state_rows, cols), F32)],
    )
    return normed, grad_in, gate_grad, grad_prompt, grad_start


def solution(mesh):
    return jax.shard_map(
        body,
        mesh=mesh,
        in_specs=(
            P("dp", "ctx", "tensor"),
            P("dp", "ctx", "tensor"),
            P("dp", "ctx", None),
            P("dp", "ctx", None),
            P("dp", "ctx", "tensor"),
            P("dp", "ctx"),
            P("tensor"),
            P("tensor"),
            P(None, "tensor"),
            P(),
            P(None, "tensor"),
            P(None, "tensor"),
            P("dp", "ctx", "tensor"),
        ),
        out_specs=(
            P("dp", "ctx", "tensor"),
            P("dp", "ctx", "tensor"),
            P("dp", "ctx", "tensor"),
            P(None, "tensor"),
            P(None, "tensor"),
        ),
        check_vma=False,
    )
```

profile of v0, /device:TPU:0, one launch (start us, length us, event | category | flops | bytes accessed | tf_op | source)
XLA Modules:
  0.0 170.0 jit_solution(12954961823929528943)
XLA Ops:
  8.5 2.6 %shard_map.164 = (f32[512,128]{1,0:T(8,128)S(1)}, bf16[512,128]{1,0:T(8,128)(2,1)S(1)}, f32[136,512]{1,0:T(8,128)S(1)}, f32[136,512]{1,0:T(8,128)S(1)}, f32[136,...) custom-call(s32[1,1]{1,0:T(1,128)S(6)} %copy.74.refs_0_, ...), custom_call_target="tpu_custom_call" | custom-call | tf_op jit(solution)/shard_map/pallas_call | solution.py:491
  11.1 4.9 %collective-permute-start = (f32[136,512]{1,0:T(8,128)S(1)}, f32[136,512]{1,0:T(8,128)S(1)}, u32[]{:S(2)}, u32[]{:S(2)}) collective-permute-start(f32[136,512]{1,0:T(8,128)S(1)} %get-tuple-element.148), channel_id=1, source_target_pairs={{0,2},{1,3},{8,10},{9,11},{16,18},{17,19},{24,26},{25,27}} | collective-permute-start | bytes 835592 | tf_op jit(solution)/shard_map/ppermute | solution.py:551
  16.0 4.9 %shard_map.169 = (f32[512,128]{1,0:T(8,128)S(1)}, bf16[512,128]{1,0:T(8,128)(2,1)S(1)}, f32[136,512]{1,0:T(8,128)S(1)}, f32[136,512]{1,0:T(8,128)S(1)}, f32[136,...) custom-call(s32[1,1]{1,0:T(1,128)S(6)} %copy.74.refs_0_, ...), custom_call_target="tpu_custom_call" | custom-call | tf_op jit(solution)/shard_map/pallas_call | solution.py:491
  23.7 4.9 %shard_map.166 = (f32[512,128]{1,0:T(8,128)S(1)}, bf16[512,128]{1,0:T(8,128)(2,1)S(1)}, f32[136,512]{1,0:T(8,128)S(1)}, f32[136,512]{1,0:T(8,128)S(1)}, f32[136,...) custom-call(s32[1,1]{1,0:T(1,128)S(6)} %copy.74.refs_0_, ...), custom_call_target="tpu_custom_call" | custom-call | tf_op jit(solution)/shard_map/pallas_call | solution.py:491
  28.7 2.7 %collective-permute-start.3 = (f32[136,512]{1,0:T(8,128)S(1)}, f32[136,512]{1,0:T(8,128)S(1)}, u32[]{:S(2)}, u32[]{:S(2)}) collective-permute-start(f32[136,512]{1,0:T(8,128)S(1)} %get-tuple-element.161), channel_id=1, source_target_pairs={{0,2},{1,3},{8,10},{9,11},{16,18},{17,19},{24,26},{25,27}} | collective-permute-start | bytes 835592 | tf_op jit(solution)/shard_map/ppermute | solution.py:551
  36.1 5.2 %collective-permute-done.3.refs_0_ = f32[136,512]{1,0:T(8,128)S(1)} collective-permute-done((f32[136,512]{1,0:T(8,128)S(1)}, f32[136,512]{1,0:T(8,128)S(1)}, u32[]{:S(2)}, u32[]{:S(2)}) %collective-permute-start.3) | collective-permute-done | bytes 278560 | tf_op jit(solution)/shard_map/ppermute | solution.py:551
  42.0 4.1 %collective-permute-done.1.refs_0_ = f32[136,512]{1,0:T(8,128)S(1)} collective-permute-done((f32[136,512]{1,0:T(8,128)S(1)}, f32[136,512]{1,0:T(8,128)S(1)}, u32[]{:S(2)}, u32[]{:S(2)}) %collective-permute-start.1) | collective-permute-done | bytes 278560 | tf_op jit(solution)/shard_map/ppermute | solution.py:551
  47.6 2.8 %shard_map.173 = (f32[512,512]{1,0:T(8,128)S(1)}, f32[136,512]{1,0:T(8,128)S(1)}) custom-call(s32[1,1]{1,0:T(1,128)S(6)} %copy.74.refs_0_, f32[512,128]{1,0:T(8,128)S(1)} %get-tuple-element.178.refs_1_, bf16[1,512,128]{2,1,0:T(8,128)(2,1)S(1)} %copy-done.3, bf16[1,512,128]{2,1,0:T(8,128)(2,1)S(1)} %copy-done.5, ...), custom_call_target="tpu_custom_call", output_to_operand_aliasing={{1}: (7, {})} | custom-call | tf_op jit(solution)/shard_map/pallas_call | solution.py:491
  51.2 2.8 %shard_map.175 = (f32[512,512]{1,0:T(8,128)S(1)}, f32[136,512]{1,0:T(8,128)S(1)}) custom-call(s32[1,1]{1,0:T(1,128)S(6)} %copy.74.refs_0_, f32[512,128]{1,0:T(8,128)S(1)} %get-tuple-element.172.refs_1_, bf16[1,512,128]{2,1,0:T(8,128)(2,1)S(1)} %copy-done.3, bf16[1,512,128]{2,1,0:T(8,128)(2,1)S(1)} %copy-done.5, ...), custom_call_target="tpu_custom_call", output_to_operand_aliasing={{1}: (7, {})} | custom-call | tf_op jit(solution)/shard_map/pallas_call | solution.py:491
  54.9 2.8 %shard_map.177 = (f32[512,512]{1,0:T(8,128)S(1)}, f32[136,512]{1,0:T(8,128)S(1)}) custom-call(s32[1,1]{1,0:T(1,128)S(6)} %copy.74.refs_0_, f32[512,128]{1,0:T(8,128)S(1)} %get-tuple-element.166.refs_1_, bf16[1,512,128]{2,1,0:T(8,128)(2,1)S(1)} %copy-done.3, bf16[1,512,128]{2,1,0:T(8,128)(2,1)S(1)} %copy-done.5, ...), custom_call_target="tpu_custom_call", output_to_operand_aliasing={{1}: (7, {})} | custom-call | tf_op jit(solution)/shard_map/pallas_call | solution.py:491
  58.5 2.8 %shard_map.179 = (f32[512,512]{1,0:T(8,128)S(1)}, f32[136,512]{1,0:T(8,128)S(1)}) custom-call(s32[1,1]{1,0:T(1,128)S(6)} %copy.74.refs_0_, f32[512,128]{1,0:T(8,128)S(1)} %get-tuple-element.160.refs_1_, bf16[1,512,128]{2,1,0:T(8,128)(2,1)S(1)} %copy-done.3, bf16[1,512,128]{2,1,0:T(8,128)(2,1)S(1)} %copy-done.5, ...), custom_call_target="tpu_custom_call", output_to_operand_aliasing={{1}: (7, {})} | custom-call | tf_op jit(solution)/shard_map/pallas_call | solution.py:491
  62.3 2.8 %shard_map.181.refs_2_ = f32[512,512]{1,0:T(8,128)S(1)} custom-call(s32[1,1]{1,0:T(1,128)S(6)} %copy.74.refs_0_, f32[512,128]{1,0:T(8,128)S(1)} %get-tuple-element.153.refs_1_, bf16[1,512,128]{2,1,0:T(8,128)(2,1)S(1)} %copy-done.3, bf16[1,512,128]{2,1,0:T(8,128)(2,1)S(1)} %copy-done.5, bf16[1,512,2560]{2,1,0:T(8,128)(2,1)S(1)} %copy-done.2, ...), custom_call_target="tpu_custom_call" | custom-call | tf_op jit(solution)/shard_map/pallas_call | solution.py:491
  72.5 7.3 %shard_map.187 = (bf16[512,2560]{1,0:T(8,128)(2,1)S(1)}, f32[128,512]{1,0:T(8,128)S(1)}, f32[128,512]{1,0:T(8,128)S(1)}, f32[128,512]{1,0:T(8,128)S(1)}, f32[128...) custom-call(s32[1,1]{1,0:T(1,128)S(6)} %copy.74.refs_0_, ...), custom_call_target="tpu_custom_call" | custom-call | tf_op jit(solution)/shard_map/pallas_call | solution.py:491
  84.1 4.7 %shard_map.188 = (f32[512,512]{1,0:T(8,128)S(1)}, bf16[1,512,2560]{2,1,0:T(8,128)(2,1)}, bf16[1,512,2560]{2,1,0:T(8,128)(2,1)}, f32[32,2560]{1,0:T(8,128)S(1)}, ...) custom-call(s32[1,1]{1,0:T(1,128)S(6)} %copy.74.refs_0_, ...), custom_call_target="tpu_custom_call", output_to_operand_aliasing={{3}: (12, {}), {4}: (13, {}), {5}: (14, {}), {6}: (15, {})} | custom-call | tf_op jit(solution)/shard_map/pallas_call | solution.py:491
  93.9 13.4 %collective-permute-done.20.refs_15_.refs_3_ = f32[128,512]{1,0:T(8,128)S(1)} collective-permute-done((f32[128,512]{1,0:T(8,128)S(1)}, f32[128,512]{1,0:T(8,128)S(1)}, u32[]{:S(2)}, u32[]{:S(2)}) %collective-permute-start.20) | collective-permute-done | bytes 262176 | tf_op jit(solution)/shard_map/ppermute | solution.py:646
  107.3 4.7 %shard_map.193 = (f32[512,512]{1,0:T(8,128)S(1)}, bf16[1,512,2560]{2,1,0:T(8,128)(2,1)}, bf16[1,512,2560]{2,1,0:T(8,128)(2,1)}) custom-call(s32[1,1]{1,0:T(1,128)S(6)} %copy.74.refs_0_, f32[512,128]{1,0:T(8,128)S(1)} %get-tuple-element.172.refs_1_, bf16[1,512,128]{2,1,0:T(8,128)(2,1)S(1)} %copy-done.4, ...), custom_call_target="tpu_custom_call", output_to_operand_aliasing={{1}: (12, {}), {2}: (13, {})} | custom-call | tf_op jit(solution)/shard_map/pallas_call | solution.py:491
  118.6 4.7 %shard_map.196 = (f32[512,512]{1,0:T(8,128)S(1)}, bf16[1,512,2560]{2,1,0:T(8,128)(2,1)}, bf16[1,512,2560]{2,1,0:T(8,128)(2,1)}) custom-call(s32[1,1]{1,0:T(1,128)S(6)} %copy.74.refs_0_, f32[512,128]{1,0:T(8,128)S(1)} %get-tuple-element.166.refs_1_, bf16[1,512,128]{2,1,0:T(8,128)(2,1)S(1)} %copy-done.4, ...), custom_call_target="tpu_custom_call", output_to_operand_aliasing={{1}: (12, {}), {2}: (13, {})} | custom-call | tf_op jit(solution)/shard_map/pallas_call | solution.py:491
  124.7 4.7 %shard_map.199 = (f32[512,512]{1,0:T(8,128)S(1)}, bf16[1,512,2560]{2,1,0:T(8,128)(2,1)}, bf16[1,512,2560]{2,1,0:T(8,128)(2,1)}) custom-call(s32[1,1]{1,0:T(1,128)S(6)} %copy.74.refs_0_, f32[512,128]{1,0:T(8,128)S(1)} %get-tuple-element.160.refs_1_, bf16[1,512,128]{2,1,0:T(8,128)(2,1)S(1)} %copy-done.4, ...), custom_call_target="tpu_custom_call", output_to_operand_aliasing={{1}: (12, {}), {2}: (13, {})} | custom-call | tf_op jit(solution)/shard_map/pallas_call | solution.py:491
  130.8 4.3 %collective-permute-done.32.refs_6_.refs_3_ = f32[128,512]{1,0:T(8,128)S(1)} collective-permute-done((f32[128,512]{1,0:T(8,128)S(1)}, f32[128,512]{1,0:T(8,128)S(1)}, u32[]{:S(2)}, u32[]{:S(2)}) %collective-permute-start.32) | collective-permute-done | bytes 262176 | tf_op jit(solution)/shard_map/ppermute | solution.py:646
  136.9 2.8 %collective-permute-start.35 = (f32[8,2560]{1,0:T(8,128)S(1)}, f32[8,2560]{1,0:T(8,128)S(1)}, u32[]{:S(2)}, u32[]{:S(2)}) collective-permute-start(f32[8,2560]{1,0:T(8,128)S(1)} %get-tuple-element.275), channel_id=1, source_target_pairs={{0,6},{2,0},{4,2},{6,4},{1,7},{3,1},{5,3},{7,5},{8,14},{10,8},{12,... | collective-permute-start | bytes 245768 | tf_op jit(solution)/shard_map/ppermute | solution.py:733
  145.0 2.3 %collective-permute-start.38 = (f32[8,2560]{1,0:T(8,128)S(1)}, f32[8,2560]{1,0:T(8,128)S(1)}, u32[]{:S(2)}, u32[]{:S(2)}) collective-permute-start(f32[8,2560]{1,0:T(8,128)S(1)} %shard_map.203.refs_14_.refs_0_), channel_id=1, source_target_pairs={{0,4},{2,6},{4,0},{6,2},{1,5},{3,7},{5,1},{7,3},{8,12},{10,14},{12... | collective-permute-start | bytes 245768 | tf_op jit(solution)/shard_map/ppermute | solution.py:737
  148.8 4.7 %shard_map.204 = (f32[512,512]{1,0:T(8,128)S(1)}, bf16[1,512,2560]{2,1,0:T(8,128)(2,1)}, bf16[1,512,2560]{2,1,0:T(8,128)(2,1)}) custom-call(s32[1,1]{1,0:T(1,128)S(6)} %copy.74.refs_0_, f32[512,128]{1,0:T(8,128)S(1)} %get-tuple-element.153.refs_1_, bf16[1,512,128]{2,1,0:T(8,128)(2,1)S(1)} %copy-done.4, ...), custom_call_target="tpu_custom_call", output_to_operand_aliasing={{1}: (12, {}), {2}: (13, {})} | custom-call | tf_op jit(solution)/shard_map/pallas_call | solution.py:491
  154.2 2.5 %collective-permute-start.41 = (f32[32,2560]{1,0:T(8,128)S(1)}, f32[32,2560]{1,0:T(8,128)S(1)}, u32[]{:S(2)}, u32[]{:S(2)}) collective-permute-start(f32[32,2560]{1,0:T(8,128)S(1)} %shard_map.210.refs_6_), channel_id=1, source_target_pairs={{0,16},{8,24},{16,0},{24,8},{1,17},{9,25},{17,1},{25,9},{2,18},{10... | collective-permute-start | bytes 983048 | tf_op jit(solution)/shard_map/ppermute | solution.py:747
  164.3 3.1 %collective-permute-done.41.refs_8_ = f32[32,2560]{1,0:T(8,128)S(1)} collective-permute-done((f32[32,2560]{1,0:T(8,128)S(1)}, f32[32,2560]{1,0:T(8,128)S(1)}, u32[]{:S(2)}, u32[]{:S(2)}) %collective-permute-start.41) | collective-permute-done | bytes 327712 | tf_op jit(solution)/shard_map/ppermute | solution.py:747
  (139 shorter events, 65.5 us)
Async XLA Ops:
  11.1 12.5 %collective-permute-start = (f32[136,512]{1,0:T(8,128)S(1)}, f32[136,512]{1,0:T(8,128)S(1)}, u32[]{:S(2)}, u32[]{:S(2)}) collective-permute-start(f32[136,512]{1,0:T(8,128)S(1)} %get-tuple-element.148), channel_id=1, source_target_pairs={{0,2},{1,3},{8,10},{9,11},{16,18},{17,19},{24,26},{25,27}} | collective-permute-start | bytes 835592 | tf_op jit(solution)/shard_map/ppermute | solution.py:551
  21.0 12.4 %collective-permute-start.7 = (f32[136,512]{1,0:T(8,128)S(1)}, f32[136,512]{1,0:T(8,128)S(1)}, u32[]{:S(2)}, u32[]{:S(2)}) collective-permute-start(f32[136,512]{1,0:T(8,128)S(1)} %get-tuple-element.173), channel_id=1, source_target_pairs={{0,2},{1,3},{8,10},{9,11},{16,18},{17,19},{24,26},{25,27}} | collective-permute-start | bytes 835592 | tf_op jit(solution)/shard_map/ppermute | solution.py:551
  22.3 13.0 %collective-permute-start.5 = (f32[136,512]{1,0:T(8,128)S(1)}, f32[136,512]{1,0:T(8,128)S(1)}, u32[]{:S(2)}, u32[]{:S(2)}) collective-permute-start(f32[136,512]{1,0:T(8,128)S(1)} %get-tuple-element.167), channel_id=1, source_target_pairs={{0,2},{1,3},{8,10},{9,11},{16,18},{17,19},{24,26},{25,27}} | collective-permute-start | bytes 835592 | tf_op jit(solution)/shard_map/ppermute | solution.py:551
  28.7 12.6 %collective-permute-start.3 = (f32[136,512]{1,0:T(8,128)S(1)}, f32[136,512]{1,0:T(8,128)S(1)}, u32[]{:S(2)}, u32[]{:S(2)}) collective-permute-start(f32[136,512]{1,0:T(8,128)S(1)} %get-tuple-element.161), channel_id=1, source_target_pairs={{0,2},{1,3},{8,10},{9,11},{16,18},{17,19},{24,26},{25,27}} | collective-permute-start | bytes 835592 | tf_op jit(solution)/shard_map/ppermute | solution.py:551
  31.4 14.7 %collective-permute-start.1 = (f32[136,512]{1,0:T(8,128)S(1)}, f32[136,512]{1,0:T(8,128)S(1)}, u32[]{:S(2)}, u32[]{:S(2)}) collective-permute-start(f32[136,512]{1,0:T(8,128)S(1)} %get-tuple-element.155), channel_id=1, source_target_pairs={{0,2},{1,3},{8,10},{9,11},{16,18},{17,19},{24,26},{25,27}} | collective-permute-start | bytes 835592 | tf_op jit(solution)/shard_map/ppermute | solution.py:551
  32.7 14.2 %collective-permute-start.9 = (f32[136,512]{1,0:T(8,128)S(1)}, f32[136,512]{1,0:T(8,128)S(1)}, u32[]{:S(2)}, u32[]{:S(2)}) collective-permute-start(f32[136,512]{1,0:T(8,128)S(1)} %get-tuple-element.152.refs_8_), channel_id=1, source_target_pairs={{2,4},{3,5},{10,12},{11,13},{18,20},{19,21},{26,28},{27,29}} | collective-permute-start | bytes 835592 | tf_op jit(solution)/shard_map/ppermute | solution.py:551
  33.5 17.0 %collective-permute-start.8 = (f32[136,512]{1,0:T(8,128)S(1)}, f32[136,512]{1,0:T(8,128)S(1)}, u32[]{:S(2)}, u32[]{:S(2)}) collective-permute-start(f32[136,512]{1,0:T(8,128)S(1)} %get-tuple-element.177), channel_id=1, source_target_pairs={{2,4},{3,5},{10,12},{11,13},{18,20},{19,21},{26,28},{27,29}} | collective-permute-start | bytes 835592 | tf_op jit(solution)/shard_map/ppermute | solution.py:551
  35.4 18.6 %collective-permute-start.6 = (f32[136,512]{1,0:T(8,128)S(1)}, f32[136,512]{1,0:T(8,128)S(1)}, u32[]{:S(2)}, u32[]{:S(2)}) collective-permute-start(f32[136,512]{1,0:T(8,128)S(1)} %get-tuple-element.171), channel_id=1, source_target_pairs={{2,4},{3,5},{10,12},{11,13},{18,20},{19,21},{26,28},{27,29}} | collective-permute-start | bytes 835592 | tf_op jit(solution)/shard_map/ppermute | solution.py:551
  41.4 16.4 %collective-permute-start.4 = (f32[136,512]{1,0:T(8,128)S(1)}, f32[136,512]{1,0:T(8,128)S(1)}, u32[]{:S(2)}, u32[]{:S(2)}) collective-permute-start(f32[136,512]{1,0:T(8,128)S(1)} %get-tuple-element.165), channel_id=1, source_target_pairs={{2,4},{3,5},{10,12},{11,13},{18,20},{19,21},{26,28},{27,29}} | collective-permute-start | bytes 835592 | tf_op jit(solution)/shard_map/ppermute | solution.py:551
  46.2 15.1 %collective-permute-start.2 = (f32[136,512]{1,0:T(8,128)S(1)}, f32[136,512]{1,0:T(8,128)S(1)}, u32[]{:S(2)}, u32[]{:S(2)}) collective-permute-start(f32[136,512]{1,0:T(8,128)S(1)} %get-tuple-element.159), channel_id=1, source_target_pairs={{2,4},{3,5},{10,12},{11,13},{18,20},{19,21},{26,28},{27,29}} | collective-permute-start | bytes 835592 | tf_op jit(solution)/shard_map/ppermute | solution.py:551
  46.9 18.1 %collective-permute-start.14 = (f32[136,512]{1,0:T(8,128)S(1)}, f32[136,512]{1,0:T(8,128)S(1)}, u32[]{:S(2)}, u32[]{:S(2)}) collective-permute-start(f32[136,512]{1,0:T(8,128)S(1)} %get-tuple-element.181.refs_6_), channel_id=1, source_target_pairs={{4,6},{5,7},{12,14},{13,15},{20,22},{21,23},{28,30},{29,31}} | collective-permute-start | bytes 835592 | tf_op jit(solution)/shard_map/ppermute | solution.py:551
  50.5 15.7 %collective-permute-start.13 = (f32[136,512]{1,0:T(8,128)S(1)}, f32[136,512]{1,0:T(8,128)S(1)}, u32[]{:S(2)}, u32[]{:S(2)}) collective-permute-start(f32[136,512]{1,0:T(8,128)S(1)} %get-tuple-element.185.refs_6_), channel_id=1, source_target_pairs={{4,6},{5,7},{12,14},{13,15},{20,22},{21,23},{28,30},{29,31}} | collective-permute-start | bytes 835592 | tf_op jit(solution)/shard_map/ppermute | solution.py:551
  54.1 13.3 %collective-permute-start.12 = (f32[136,512]{1,0:T(8,128)S(1)}, f32[136,512]{1,0:T(8,128)S(1)}, u32[]{:S(2)}, u32[]{:S(2)}) collective-permute-start(f32[136,512]{1,0:T(8,128)S(1)} %get-tuple-element.189.refs_6_), channel_id=1, source_target_pairs={{4,6},{5,7},{12,14},{13,15},{20,22},{21,23},{28,30},{29,31}} | collective-permute-start | bytes 835592 | tf_op jit(solution)/shard_map/ppermute | solution.py:551
  88.8 18.5 %collective-permute-start.20 = (f32[128,512]{1,0:T(8,128)S(1)}, f32[128,512]{1,0:T(8,128)S(1)}, u32[]{:S(2)}, u32[]{:S(2)}) collective-permute-start(f32[128,512]{1,0:T(8,128)S(1)} %get-tuple-element.246), channel_id=1, source_target_pairs={{2,0},{3,1},{10,8},{11,9},{18,16},{19,17},{26,24},{27,25}} | collective-permute-start | bytes 786440 | tf_op jit(solution)/shard_map/ppermute | solution.py:646
  90.2 21.8 %collective-permute-start.22 = (f32[128,512]{1,0:T(8,128)S(1)}, f32[128,512]{1,0:T(8,128)S(1)}, u32[]{:S(2)}, u32[]{:S(2)}) collective-permute-start(f32[128,512]{1,0:T(8,128)S(1)} %get-tuple-element.250), channel_id=1, source_target_pairs={{4,2},{5,3},{12,10},{13,11},{20,18},{21,19},{28,26},{29,27}} | collective-permute-start | bytes 786440 | tf_op jit(solution)/shard_map/ppermute | solution.py:646
  90.9 22.5 %collective-permute-start.30 = (f32[128,512]{1,0:T(8,128)S(1)}, f32[128,512]{1,0:T(8,128)S(1)}, u32[]{:S(2)}, u32[]{:S(2)}) collective-permute-start(f32[128,512]{1,0:T(8,128)S(1)} %get-tuple-element.267.refs_1_), channel_id=1, source_target_pairs={{6,4},{7,5},{14,12},{15,13},{22,20},{23,21},{30,28},{31,29}} | collective-permute-start | bytes 786440 | tf_op jit(solution)/shard_map/ppermute | solution.py:646
  91.6 24.0 %collective-permute-start.25 = (f32[128,512]{1,0:T(8,128)S(1)}, f32[128,512]{1,0:T(8,128)S(1)}, u32[]{:S(2)}, u32[]{:S(2)}) collective-permute-start(f32[128,512]{1,0:T(8,128)S(1)} %get-tuple-element.257), channel_id=1, source_target_pairs={{4,2},{5,3},{12,10},{13,11},{20,18},{21,19},{28,26},{29,27}} | collective-permute-start | bytes 786440 | tf_op jit(solution)/shard_map/ppermute | solution.py:646
  92.4 24.8 %collective-permute-start.23 = (f32[128,512]{1,0:T(8,128)S(1)}, f32[128,512]{1,0:T(8,128)S(1)}, u32[]{:S(2)}, u32[]{:S(2)}) collective-permute-start(f32[128,512]{1,0:T(8,128)S(1)} %get-tuple-element.242.refs_14_), channel_id=1, source_target_pairs={{2,0},{3,1},{10,8},{11,9},{18,16},{19,17},{26,24},{27,25}} | collective-permute-start | bytes 786440 | tf_op jit(solution)/shard_map/ppermute | solution.py:646
  113.4 15.9 %collective-permute-start.31 = (f32[128,512]{1,0:T(8,128)S(1)}, f32[128,512]{1,0:T(8,128)S(1)}, u32[]{:S(2)}, u32[]{:S(2)}) collective-permute-start(f32[128,512]{1,0:T(8,128)S(1)} %get-tuple-element.268), channel_id=1, source_target_pairs={{4,2},{5,3},{12,10},{13,11},{20,18},{21,19},{28,26},{29,27}} | collective-permute-start | bytes 786440 | tf_op jit(solution)/shard_map/ppermute | solution.py:646
  114.1 16.6 %collective-permute-start.27 = (f32[32,2560]{1,0:T(8,128)S(1)}, f32[32,2560]{1,0:T(8,128)S(1)}, u32[]{:S(2)}, u32[]{:S(2)}) collective-permute-start(f32[32,2560]{1,0:T(8,128)S(1)} %get-tuple-element.264), channel_id=1, source_target_pairs={{0,8},{8,16},{16,24},{24,0},{1,9},{9,17},{17,25},{25,1},{2,10},{10... | collective-permute-start | bytes 983048 | tf_op jit(solution)/shard_map/ppermute | solution.py:712
  115.6 15.1 %collective-permute-start.28 = (f32[32,2560]{1,0:T(8,128)S(1)}, f32[32,2560]{1,0:T(8,128)S(1)}, u32[]{:S(2)}, u32[]{:S(2)}) collective-permute-start(f32[32,2560]{1,0:T(8,128)S(1)} %get-tuple-element.265), channel_id=1, source_target_pairs={{0,16},{8,24},{16,0},{24,8},{1,17},{9,25},{17,1},{25,9},{2,18},{10... | collective-permute-start | bytes 983048 | tf_op jit(solution)/shard_map/ppermute | solution.py:712
  117.2 13.6 %collective-permute-start.29 = (f32[32,2560]{1,0:T(8,128)S(1)}, f32[32,2560]{1,0:T(8,128)S(1)}, u32[]{:S(2)}, u32[]{:S(2)}) collective-permute-start(f32[32,2560]{1,0:T(8,128)S(1)} %get-tuple-element.266), channel_id=1, source_target_pairs={{0,24},{8,0},{16,8},{24,16},{1,25},{9,1},{17,9},{25,17},{2,26},{10... | collective-permute-start | bytes 983048 | tf_op jit(solution)/shard_map/ppermute | solution.py:712
  129.4 19.4 %collective-permute-start.36 = (f32[128,512]{1,0:T(8,128)S(1)}, f32[128,512]{1,0:T(8,128)S(1)}, u32[]{:S(2)}, u32[]{:S(2)}) collective-permute-start(f32[128,512]{1,0:T(8,128)S(1)} %get-tuple-element.271.refs_4_), channel_id=1, source_target_pairs={{2,0},{3,1},{10,8},{11,9},{18,16},{19,17},{26,24},{27,25}} | collective-permute-start | bytes 786440 | tf_op jit(solution)/shard_map/ppermute | solution.py:646
  154.2 13.2 %collective-permute-start.41 = (f32[32,2560]{1,0:T(8,128)S(1)}, f32[32,2560]{1,0:T(8,128)S(1)}, u32[]{:S(2)}, u32[]{:S(2)}) collective-permute-start(f32[32,2560]{1,0:T(8,128)S(1)} %shard_map.210.refs_6_), channel_id=1, source_target_pairs={{0,16},{8,24},{16,0},{24,8},{1,17},{9,25},{17,1},{25,9},{2,18},{10... | collective-permute-start | bytes 983048 | tf_op jit(solution)/shard_map/ppermute | solution.py:747
  (33 other events, 213.3 us)
where the time goes:
time: 171 us; the launch traced here: 170 us
  Pallas kernels  72.4 us (42%)
  starting transfers between devices  49.3 us (29%)
  waiting for transfers between devices  39 us (23%)
  local copies, waits for them, and re-layouts  7.21 us (4%)
  between operations  1.99 us (1%)
    pallas_call x48, Pallas kernels, run(): call(ordered, [whole(s) if spec is None else spec for s, spec in results]...  72.4 us
    ppermute x15, starting transfers between devices, edge_up(): return lax.ppermute(array, 'ctx', [(edge, edge + 1)])  18.6 us
    ppermute x15, waiting for transfers between devices, edge_down(): return lax.ppermute(array, 'ctx', [(edge, edge - 1)])  17.7 us
    ppermute x15, starting transfers between devices, edge_down(): return lax.ppermute(array, 'ctx', [(edge, edge - 1)])  13.5 us
    ppermute x15, waiting for transfers between devices, edge_up(): return lax.ppermute(array, 'ctx', [(edge, edge + 1)])  10.5 us
    unnamed x28, local copies, waits for them, and re-layouts  7.2 us
    ppermute x3, waiting for transfers between devices, body(): lax.ppermute(mine[d], 'ctx', ring(count, d))  5.15 us
    ppermute x3, starting transfers between devices, body(): lax.ppermute(mine[d], 'ctx', ring(count, d))  4.58 us
  transfers between devices with their start and end apart: 43, of which 12 were waited for; matrix products, arithmetic and copies ran while one was open for 0% of the time, Pallas kernels for 35%

commit v1 on v0

--- a/solution.py
+++ b/solution.py
@@ -532,7 +532,7 @@
             after=after,
             scratch=[pltpu.VMEM(b, a.dtype) for b, (a, _) in zip(blocks, ins)]
             + [pltpu.SemaphoreType.DMA((len(ins),))],
-            limit=PLIM,
+            limit=60 if ks[0] == 0 else PLIM,
         )
         for place, k in enumerate(ks):
             for held, one in zip(made, out[place * len(made) :]):

time: 171 us -> 168 us (0.982)
  local copies, waits for them, and re-layouts: 7.21 us -> 1.9 us
  Pallas kernels: 72.4 us -> 75 us
    unnamed x28 -> x44, local copies, waits for them, and re-layouts: 7.2 us -> 1.89 us
    pallas_call x48, Pallas kernels: 72.4 us -> 75 us  [run(): call(ordered, [whole(s) if spec is None else spec for s, spec in results]...]
  transfers between devices with their start and end apart: 43 -> 43, of which waited for: 12 -> 12; matrix products, arithmetic and copies ran while one was open for 0% -> 0% of each run, Pallas kernels for 35% -> 36%
where the time goes in v1:
time: 168 us; the launch traced here: 167 us
  Pallas kernels  75 us (45%)
  starting transfers between devices  48.2 us (29%)
  waiting for transfers between devices  39.7 us (24%)
  between operations  2.29 us (1%)
  local copies, waits for them, and re-layouts  1.9 us (1%)
    pallas_call x48, Pallas kernels, run(): call(ordered, [whole(s) if spec is None else spec for s, spec in results]...  75 us
    ppermute x15, starting transfers between devices, edge_up(): return lax.ppermute(array, 'ctx', [(edge, edge + 1)])  17.6 us
    ppermute x15, waiting for transfers between devices, edge_down(): return lax.ppermute(array, 'ctx', [(edge, edge - 1)])  17.3 us
    ppermute x15, starting transfers between devices, edge_down(): return lax.ppermute(array, 'ctx', [(edge, edge - 1)])  13.5 us
    ppermute x15, waiting for transfers between devices, edge_up(): return lax.ppermute(array, 'ctx', [(edge, edge + 1)])  11.5 us
    ppermute x3, waiting for transfers between devices, body(): lax.ppermute(mine[d], 'ctx', ring(count, d))  5.16 us
    ppermute x3, starting transfers between devices, body(): lax.ppermute(mine[d], 'ctx', ring(count, d))  4.52 us
    ppermute x3, starting transfers between devices, body(): lax.ppermute(parts[d], 'dp', ring(groups, d))  4.5 us
  transfers between devices with their start and end apart: 43, of which 12 were waited for; matrix products, arithmetic and copies ran while one was open for 0% of the time, Pallas kernels for 36%

profile of v1, /device:TPU:0, one launch (start us, length us, event | category | flops | bytes accessed | tf_op | source)
XLA Modules:
  0.0 167.2 jit_solution(11120114835327409424)
XLA Ops:
  1.5 5.1 %shard_map.164 = (f32[512,128]{1,0:T(8,128)}, bf16[512,128]{1,0:T(8,128)(2,1)}, f32[136,512]{1,0:T(8,128)}, f32[136,512]{1,0:T(8,128)}, f32[136,512]{1,0:T(8,128...) custom-call(s32[1,1]{1,0:T(1,128)S(6)} %copy.74.refs_0_, ...), custom_call_target="tpu_custom_call" | custom-call | tf_op jit(solution)/shard_map/pallas_call | solution.py:491
  6.6 5.1 %collective-permute-start = (f32[136,512]{1,0:T(8,128)}, f32[136,512]{1,0:T(8,128)S(1)}, u32[]{:S(2)}, u32[]{:S(2)}) collective-permute-start(f32[136,512]{1,0:T(8,128)} %get-tuple-element.148), channel_id=1, source_target_pairs={{0,2},{1,3},{8,10},{9,11},{16,18},{17,19},{24,26},{25,27}} | collective-permute-start | bytes 835592 | tf_op jit(solution)/shard_map/ppermute | solution.py:551
  13.5 4.9 %shard_map.169 = (f32[512,128]{1,0:T(8,128)S(1)}, bf16[512,128]{1,0:T(8,128)(2,1)S(1)}, f32[136,512]{1,0:T(8,128)S(1)}, f32[136,512]{1,0:T(8,128)S(1)}, f32[136,...) custom-call(s32[1,1]{1,0:T(1,128)S(6)} %copy.74.refs_0_, ...), custom_call_target="tpu_custom_call" | custom-call | tf_op jit(solution)/shard_map/pallas_call | solution.py:491
  21.3 4.9 %shard_map.166 = (f32[512,128]{1,0:T(8,128)S(1)}, bf16[512,128]{1,0:T(8,128)(2,1)S(1)}, f32[136,512]{1,0:T(8,128)S(1)}, f32[136,512]{1,0:T(8,128)S(1)}, f32[136,...) custom-call(s32[1,1]{1,0:T(1,128)S(6)} %copy.74.refs_0_, ...), custom_call_target="tpu_custom_call" | custom-call | tf_op jit(solution)/shard_map/pallas_call | solution.py:491
  30.6 2.2 %collective-permute-done.5.refs_0_ = f32[136,512]{1,0:T(8,128)S(1)} collective-permute-done((f32[136,512]{1,0:T(8,128)S(1)}, f32[136,512]{1,0:T(8,128)S(1)}, u32[]{:S(2)}, u32[]{:S(2)}) %collective-permute-start.5) | collective-permute-done | bytes 278560 | tf_op jit(solution)/shard_map/ppermute | solution.py:551
  33.5 5.2 %collective-permute-done.3.refs_0_ = f32[136,512]{1,0:T(8,128)S(1)} collective-permute-done((f32[136,512]{1,0:T(8,128)S(1)}, f32[136,512]{1,0:T(8,128)S(1)}, u32[]{:S(2)}, u32[]{:S(2)}) %collective-permute-start.3) | collective-permute-done | bytes 278560 | tf_op jit(solution)/shard_map/ppermute | solution.py:551
  39.5 4.1 %collective-permute-done.1.refs_0_ = f32[136,512]{1,0:T(8,128)S(1)} collective-permute-done((f32[136,512]{1,0:T(8,128)S(1)}, f32[136,512]{1,0:T(8,128)S(1)}, u32[]{:S(2)}, u32[]{:S(2)}) %collective-permute-start.1) | collective-permute-done | bytes 278560 | tf_op jit(solution)/shard_map/ppermute | solution.py:551
  45.1 2.8 %shard_map.173 = (f32[512,512]{1,0:T(8,128)S(1)}, f32[136,512]{1,0:T(8,128)S(1)}) custom-call(s32[1,1]{1,0:T(1,128)S(6)} %copy.74.refs_0_, f32[512,128]{1,0:T(8,128)S(1)} %copy-done.10, bf16[1,512,128]{2,1,0:T(8,128)(2,1)S(1)} %copy-done.3, bf16[1,512,128]{2,1,0:T(8,128)(2,1)S(1)} %copy-done.4, ...), custom_call_target="tpu_custom_call", output_to_operand_aliasing={{1}: (7, {})} | custom-call | tf_op jit(solution)/shard_map/pallas_call | solution.py:491
  48.7 2.8 %shard_map.175 = (f32[512,512]{1,0:T(8,128)S(1)}, f32[136,512]{1,0:T(8,128)S(1)}) custom-call(s32[1,1]{1,0:T(1,128)S(6)} %copy.74.refs_0_, f32[512,128]{1,0:T(8,128)S(1)} %get-tuple-element.172.refs_1_, bf16[1,512,128]{2,1,0:T(8,128)(2,1)S(1)} %copy-done.3, bf16[1,512,128]{2,1,0:T(8,128)(2,1)S(1)} %copy-done.4, ...), custom_call_target="tpu_custom_call", output_to_operand_aliasing={{1}: (7, {})} | custom-call | tf_op jit(solution)/shard_map/pallas_call | solution.py:491
  52.4 2.8 %shard_map.177 = (f32[512,512]{1,0:T(8,128)S(1)}, f32[136,512]{1,0:T(8,128)S(1)}) custom-call(s32[1,1]{1,0:T(1,128)S(6)} %copy.74.refs_0_, f32[512,128]{1,0:T(8,128)S(1)} %get-tuple-element.166.refs_1_, bf16[1,512,128]{2,1,0:T(8,128)(2,1)S(1)} %copy-done.3, bf16[1,512,128]{2,1,0:T(8,128)(2,1)S(1)} %copy-done.4, ...), custom_call_target="tpu_custom_call", output_to_operand_aliasing={{1}: (7, {})} | custom-call | tf_op jit(solution)/shard_map/pallas_call | solution.py:491
  56.0 2.8 %shard_map.179 = (f32[512,512]{1,0:T(8,128)S(1)}, f32[136,512]{1,0:T(8,128)S(1)}) custom-call(s32[1,1]{1,0:T(1,128)S(6)} %copy.74.refs_0_, f32[512,128]{1,0:T(8,128)S(1)} %get-tuple-element.160.refs_1_, bf16[1,512,128]{2,1,0:T(8,128)(2,1)S(1)} %copy-done.3, bf16[1,512,128]{2,1,0:T(8,128)(2,1)S(1)} %copy-done.4, ...), custom_call_target="tpu_custom_call", output_to_operand_aliasing={{1}: (7, {})} | custom-call | tf_op jit(solution)/shard_map/pallas_call | solution.py:491
  59.8 2.8 %shard_map.181.refs_2_ = f32[512,512]{1,0:T(8,128)S(1)} custom-call(s32[1,1]{1,0:T(1,128)S(6)} %copy.74.refs_0_, f32[512,128]{1,0:T(8,128)S(1)} %get-tuple-element.153.refs_1_, bf16[1,512,128]{2,1,0:T(8,128)(2,1)S(1)} %copy-done.3, bf16[1,512,128]{2,1,0:T(8,128)(2,1)S(1)} %copy-done.4, bf16[1,512,2560]{2,1,0:T(8,128)(2,1)S(1)} %copy-done.2, ...), custom_call_target="tpu_custom_call" | custom-call | tf_op jit(solution)/shard_map/pallas_call | solution.py:491
  70.0 7.3 %shard_map.187 = (bf16[512,2560]{1,0:T(8,128)(2,1)S(1)}, f32[128,512]{1,0:T(8,128)S(1)}, f32[128,512]{1,0:T(8,128)S(1)}, f32[128,512]{1,0:T(8,128)S(1)}, f32[128...) custom-call(s32[1,1]{1,0:T(1,128)S(6)} %copy.74.refs_0_, ...), custom_call_target="tpu_custom_call" | custom-call | tf_op jit(solution)/shard_map/pallas_call | solution.py:491
  81.6 4.7 %shard_map.188 = (f32[512,512]{1,0:T(8,128)S(1)}, bf16[1,512,2560]{2,1,0:T(8,128)(2,1)}, bf16[1,512,2560]{2,1,0:T(8,128)(2,1)}, f32[32,2560]{1,0:T(8,128)S(1)}, ...) custom-call(s32[1,1]{1,0:T(1,128)S(6)} %copy.74.refs_0_, ...), custom_call_target="tpu_custom_call", output_to_operand_aliasing={{3}: (12, {}), {4}: (13, {}), {5}: (14, {}), {6}: (15, {})} | custom-call | tf_op jit(solution)/shard_map/pallas_call | solution.py:491
  91.5 13.0 %collective-permute-done.20.refs_15_.refs_3_ = f32[128,512]{1,0:T(8,128)S(1)} collective-permute-done((f32[128,512]{1,0:T(8,128)S(1)}, f32[128,512]{1,0:T(8,128)S(1)}, u32[]{:S(2)}, u32[]{:S(2)}) %collective-permute-start.20) | collective-permute-done | bytes 262176 | tf_op jit(solution)/shard_map/ppermute | solution.py:646
  104.5 4.7 %shard_map.193 = (f32[512,512]{1,0:T(8,128)S(1)}, bf16[1,512,2560]{2,1,0:T(8,128)(2,1)}, bf16[1,512,2560]{2,1,0:T(8,128)(2,1)}) custom-call(s32[1,1]{1,0:T(1,128)S(6)} %copy.74.refs_0_, f32[512,128]{1,0:T(8,128)S(1)} %get-tuple-element.172.refs_1_, bf16[1,512,128]{2,1,0:T(8,128)(2,1)S(1)} %copy-done.3, ...), custom_call_target="tpu_custom_call", output_to_operand_aliasing={{1}: (12, {}), {2}: (13, {})} | custom-call | tf_op jit(solution)/shard_map/pallas_call | solution.py:491
  115.8 4.7 %shard_map.196 = (f32[512,512]{1,0:T(8,128)S(1)}, bf16[1,512,2560]{2,1,0:T(8,128)(2,1)}, bf16[1,512,2560]{2,1,0:T(8,128)(2,1)}) custom-call(s32[1,1]{1,0:T(1,128)S(6)} %copy.74.refs_0_, f32[512,128]{1,0:T(8,128)S(1)} %get-tuple-element.166.refs_1_, bf16[1,512,128]{2,1,0:T(8,128)(2,1)S(1)} %copy-done.3, ...), custom_call_target="tpu_custom_call", output_to_operand_aliasing={{1}: (12, {}), {2}: (13, {})} | custom-call | tf_op jit(solution)/shard_map/pallas_call | solution.py:491
  121.9 4.7 %shard_map.199 = (f32[512,512]{1,0:T(8,128)S(1)}, bf16[1,512,2560]{2,1,0:T(8,128)(2,1)}, bf16[1,512,2560]{2,1,0:T(8,128)(2,1)}) custom-call(s32[1,1]{1,0:T(1,128)S(6)} %copy.74.refs_0_, f32[512,128]{1,0:T(8,128)S(1)} %get-tuple-element.160.refs_1_, bf16[1,512,128]{2,1,0:T(8,128)(2,1)S(1)} %copy-done.3, ...), custom_call_target="tpu_custom_call", output_to_operand_aliasing={{1}: (12, {}), {2}: (13, {})} | custom-call | tf_op jit(solution)/shard_map/pallas_call | solution.py:491
  128.0 4.4 %collective-permute-done.32.refs_6_.refs_3_ = f32[128,512]{1,0:T(8,128)S(1)} collective-permute-done((f32[128,512]{1,0:T(8,128)S(1)}, f32[128,512]{1,0:T(8,128)S(1)}, u32[]{:S(2)}, u32[]{:S(2)}) %collective-permute-start.32) | collective-permute-done | bytes 262176 | tf_op jit(solution)/shard_map/ppermute | solution.py:646
  134.1 2.8 %collective-permute-start.35 = (f32[8,2560]{1,0:T(8,128)S(1)}, f32[8,2560]{1,0:T(8,128)S(1)}, u32[]{:S(2)}, u32[]{:S(2)}) collective-permute-start(f32[8,2560]{1,0:T(8,128)S(1)} %get-tuple-element.275), channel_id=1, source_target_pairs={{0,6},{2,0},{4,2},{6,4},{1,7},{3,1},{5,3},{7,5},{8,14},{10,8},{12,... | collective-permute-start | bytes 245768 | tf_op jit(solution)/shard_map/ppermute | solution.py:733
  142.2 2.2 %collective-permute-start.38 = (f32[8,2560]{1,0:T(8,128)S(1)}, f32[8,2560]{1,0:T(8,128)S(1)}, u32[]{:S(2)}, u32[]{:S(2)}) collective-permute-start(f32[8,2560]{1,0:T(8,128)S(1)} %shard_map.203.refs_14_.refs_0_), channel_id=1, source_target_pairs={{0,4},{2,6},{4,0},{6,2},{1,5},{3,7},{5,1},{7,3},{8,12},{10,14},{12... | collective-permute-start | bytes 245768 | tf_op jit(solution)/shard_map/ppermute | solution.py:737
  146.0 4.7 %shard_map.204 = (f32[512,512]{1,0:T(8,128)S(1)}, bf16[1,512,2560]{2,1,0:T(8,128)(2,1)}, bf16[1,512,2560]{2,1,0:T(8,128)(2,1)}) custom-call(s32[1,1]{1,0:T(1,128)S(6)} %copy.74.refs_0_, f32[512,128]{1,0:T(8,128)S(1)} %get-tuple-element.153.refs_1_, bf16[1,512,128]{2,1,0:T(8,128)(2,1)S(1)} %copy-done.3, ...), custom_call_target="tpu_custom_call", output_to_operand_aliasing={{1}: (12, {}), {2}: (13, {})} | custom-call | tf_op jit(solution)/shard_map/pallas_call | solution.py:491
  151.4 2.5 %collective-permute-start.41 = (f32[32,2560]{1,0:T(8,128)S(1)}, f32[32,2560]{1,0:T(8,128)S(1)}, u32[]{:S(2)}, u32[]{:S(2)}) collective-permute-start(f32[32,2560]{1,0:T(8,128)S(1)} %shard_map.210.refs_6_), channel_id=1, source_target_pairs={{0,16},{8,24},{16,0},{24,8},{1,17},{9,25},{17,1},{25,9},{2,18},{10... | collective-permute-start | bytes 983048 | tf_op jit(solution)/shard_map/ppermute | solution.py:747
  161.6 3.4 %collective-permute-done.41.refs_8_ = f32[32,2560]{1,0:T(8,128)S(1)} collective-permute-done((f32[32,2560]{1,0:T(8,128)S(1)}, f32[32,2560]{1,0:T(8,128)S(1)}, u32[]{:S(2)}, u32[]{:S(2)}) %collective-permute-start.41) | collective-permute-done | bytes 327712 | tf_op jit(solution)/shard_map/ppermute | solution.py:747
  (155 shorter events, 60.4 us)
Async XLA Ops:
  6.6 14.5 %collective-permute-start = (f32[136,512]{1,0:T(8,128)}, f32[136,512]{1,0:T(8,128)S(1)}, u32[]{:S(2)}, u32[]{:S(2)}) collective-permute-start(f32[136,512]{1,0:T(8,128)} %get-tuple-element.148), channel_id=1, source_target_pairs={{0,2},{1,3},{8,10},{9,11},{16,18},{17,19},{24,26},{25,27}} | collective-permute-start | bytes 835592 | tf_op jit(solution)/shard_map/ppermute | solution.py:551
  19.8 13.0 %collective-permute-start.5 = (f32[136,512]{1,0:T(8,128)S(1)}, f32[136,512]{1,0:T(8,128)S(1)}, u32[]{:S(2)}, u32[]{:S(2)}) collective-permute-start(f32[136,512]{1,0:T(8,128)S(1)} %get-tuple-element.167), channel_id=1, source_target_pairs={{0,2},{1,3},{8,10},{9,11},{16,18},{17,19},{24,26},{25,27}} | collective-permute-start | bytes 835592 | tf_op jit(solution)/shard_map/ppermute | solution.py:551
  26.2 12.5 %collective-permute-start.3 = (f32[136,512]{1,0:T(8,128)S(1)}, f32[136,512]{1,0:T(8,128)S(1)}, u32[]{:S(2)}, u32[]{:S(2)}) collective-permute-start(f32[136,512]{1,0:T(8,128)S(1)} %get-tuple-element.161), channel_id=1, source_target_pairs={{0,2},{1,3},{8,10},{9,11},{16,18},{17,19},{24,26},{25,27}} | collective-permute-start | bytes 835592 | tf_op jit(solution)/shard_map/ppermute | solution.py:551
  27.7 15.9 %collective-permute-start.1 = (f32[136,512]{1,0:T(8,128)S(1)}, f32[136,512]{1,0:T(8,128)S(1)}, u32[]{:S(2)}, u32[]{:S(2)}) collective-permute-start(f32[136,512]{1,0:T(8,128)S(1)} %get-tuple-element.155), channel_id=1, source_target_pairs={{0,2},{1,3},{8,10},{9,11},{16,18},{17,19},{24,26},{25,27}} | collective-permute-start | bytes 835592 | tf_op jit(solution)/shard_map/ppermute | solution.py:551
  29.0 15.3 %collective-permute-start.9 = (f32[136,512]{1,0:T(8,128)S(1)}, f32[136,512]{1,0:T(8,128)S(1)}, u32[]{:S(2)}, u32[]{:S(2)}) collective-permute-start(f32[136,512]{1,0:T(8,128)S(1)} %get-tuple-element.152.refs_8_), channel_id=1, source_target_pairs={{2,4},{3,5},{10,12},{11,13},{18,20},{19,21},{26,28},{27,29}} | collective-permute-start | bytes 835592 | tf_op jit(solution)/shard_map/ppermute | solution.py:551
  29.8 18.1 %collective-permute-start.8 = (f32[136,512]{1,0:T(8,128)S(1)}, f32[136,512]{1,0:T(8,128)S(1)}, u32[]{:S(2)}, u32[]{:S(2)}) collective-permute-start(f32[136,512]{1,0:T(8,128)S(1)} %get-tuple-element.177), channel_id=1, source_target_pairs={{2,4},{3,5},{10,12},{11,13},{18,20},{19,21},{26,28},{27,29}} | collective-permute-start | bytes 835592 | tf_op jit(solution)/shard_map/ppermute | solution.py:551
  32.8 18.6 %collective-permute-start.6 = (f32[136,512]{1,0:T(8,128)S(1)}, f32[136,512]{1,0:T(8,128)S(1)}, u32[]{:S(2)}, u32[]{:S(2)}) collective-permute-start(f32[136,512]{1,0:T(8,128)S(1)} %get-tuple-element.171), channel_id=1, source_target_pairs={{2,4},{3,5},{10,12},{11,13},{18,20},{19,21},{26,28},{27,29}} | collective-permute-start | bytes 835592 | tf_op jit(solution)/shard_map/ppermute | solution.py:551
  38.8 16.4 %collective-permute-start.4 = (f32[136,512]{1,0:T(8,128)S(1)}, f32[136,512]{1,0:T(8,128)S(1)}, u32[]{:S(2)}, u32[]{:S(2)}) collective-permute-start(f32[136,512]{1,0:T(8,128)S(1)} %get-tuple-element.165), channel_id=1, source_target_pairs={{2,4},{3,5},{10,12},{11,13},{18,20},{19,21},{26,28},{27,29}} | collective-permute-start | bytes 835592 | tf_op jit(solution)/shard_map/ppermute | solution.py:551
  43.6 15.2 %collective-permute-start.2 = (f32[136,512]{1,0:T(8,128)S(1)}, f32[136,512]{1,0:T(8,128)S(1)}, u32[]{:S(2)}, u32[]{:S(2)}) collective-permute-start(f32[136,512]{1,0:T(8,128)S(1)} %get-tuple-element.159), channel_id=1, source_target_pairs={{2,4},{3,5},{10,12},{11,13},{18,20},{19,21},{26,28},{27,29}} | collective-permute-start | bytes 835592 | tf_op jit(solution)/shard_map/ppermute | solution.py:551
  44.4 18.2 %collective-permute-start.14 = (f32[136,512]{1,0:T(8,128)S(1)}, f32[136,512]{1,0:T(8,128)S(1)}, u32[]{:S(2)}, u32[]{:S(2)}) collective-permute-start(f32[136,512]{1,0:T(8,128)S(1)} %get-tuple-element.181.refs_6_), channel_id=1, source_target_pairs={{4,6},{5,7},{12,14},{13,15},{20,22},{21,23},{28,30},{29,31}} | collective-permute-start | bytes 835592 | tf_op jit(solution)/shard_map/ppermute | solution.py:551
  48.0 15.8 %collective-permute-start.13 = (f32[136,512]{1,0:T(8,128)S(1)}, f32[136,512]{1,0:T(8,128)S(1)}, u32[]{:S(2)}, u32[]{:S(2)}) collective-permute-start(f32[136,512]{1,0:T(8,128)S(1)} %get-tuple-element.185.refs_6_), channel_id=1, source_target_pairs={{4,6},{5,7},{12,14},{13,15},{20,22},{21,23},{28,30},{29,31}} | collective-permute-start | bytes 835592 | tf_op jit(solution)/shard_map/ppermute | solution.py:551
  51.6 13.4 %collective-permute-start.12 = (f32[136,512]{1,0:T(8,128)S(1)}, f32[136,512]{1,0:T(8,128)S(1)}, u32[]{:S(2)}, u32[]{:S(2)}) collective-permute-start(f32[136,512]{1,0:T(8,128)S(1)} %get-tuple-element.189.refs_6_), channel_id=1, source_target_pairs={{4,6},{5,7},{12,14},{13,15},{20,22},{21,23},{28,30},{29,31}} | collective-permute-start | bytes 835592 | tf_op jit(solution)/shard_map/ppermute | solution.py:551
  86.4 18.1 %collective-permute-start.20 = (f32[128,512]{1,0:T(8,128)S(1)}, f32[128,512]{1,0:T(8,128)S(1)}, u32[]{:S(2)}, u32[]{:S(2)}) collective-permute-start(f32[128,512]{1,0:T(8,128)S(1)} %get-tuple-element.246), channel_id=1, source_target_pairs={{2,0},{3,1},{10,8},{11,9},{18,16},{19,17},{26,24},{27,25}} | collective-permute-start | bytes 786440 | tf_op jit(solution)/shard_map/ppermute | solution.py:646
  87.8 21.4 %collective-permute-start.22 = (f32[128,512]{1,0:T(8,128)S(1)}, f32[128,512]{1,0:T(8,128)S(1)}, u32[]{:S(2)}, u32[]{:S(2)}) collective-permute-start(f32[128,512]{1,0:T(8,128)S(1)} %get-tuple-element.250), channel_id=1, source_target_pairs={{4,2},{5,3},{12,10},{13,11},{20,18},{21,19},{28,26},{29,27}} | collective-permute-start | bytes 786440 | tf_op jit(solution)/shard_map/ppermute | solution.py:646
  88.5 22.1 %collective-permute-start.30 = (f32[128,512]{1,0:T(8,128)S(1)}, f32[128,512]{1,0:T(8,128)S(1)}, u32[]{:S(2)}, u32[]{:S(2)}) collective-permute-start(f32[128,512]{1,0:T(8,128)S(1)} %get-tuple-element.267.refs_1_), channel_id=1, source_target_pairs={{6,4},{7,5},{14,12},{15,13},{22,20},{23,21},{30,28},{31,29}} | collective-permute-start | bytes 786440 | tf_op jit(solution)/shard_map/ppermute | solution.py:646
  89.2 23.6 %collective-permute-start.25 = (f32[128,512]{1,0:T(8,128)S(1)}, f32[128,512]{1,0:T(8,128)S(1)}, u32[]{:S(2)}, u32[]{:S(2)}) collective-permute-start(f32[128,512]{1,0:T(8,128)S(1)} %get-tuple-element.257), channel_id=1, source_target_pairs={{4,2},{5,3},{12,10},{13,11},{20,18},{21,19},{28,26},{29,27}} | collective-permute-start | bytes 786440 | tf_op jit(solution)/shard_map/ppermute | solution.py:646
  90.0 24.4 %collective-permute-start.23 = (f32[128,512]{1,0:T(8,128)S(1)}, f32[128,512]{1,0:T(8,128)S(1)}, u32[]{:S(2)}, u32[]{:S(2)}) collective-permute-start(f32[128,512]{1,0:T(8,128)S(1)} %get-tuple-element.242.refs_14_), channel_id=1, source_target_pairs={{2,0},{3,1},{10,8},{11,9},{18,16},{19,17},{26,24},{27,25}} | collective-permute-start | bytes 786440 | tf_op jit(solution)/shard_map/ppermute | solution.py:646
  110.6 16.0 %collective-permute-start.31 = (f32[128,512]{1,0:T(8,128)S(1)}, f32[128,512]{1,0:T(8,128)S(1)}, u32[]{:S(2)}, u32[]{:S(2)}) collective-permute-start(f32[128,512]{1,0:T(8,128)S(1)} %get-tuple-element.268), channel_id=1, source_target_pairs={{4,2},{5,3},{12,10},{13,11},{20,18},{21,19},{28,26},{29,27}} | collective-permute-start | bytes 786440 | tf_op jit(solution)/shard_map/ppermute | solution.py:646
  111.3 16.6 %collective-permute-start.27 = (f32[32,2560]{1,0:T(8,128)S(1)}, f32[32,2560]{1,0:T(8,128)S(1)}, u32[]{:S(2)}, u32[]{:S(2)}) collective-permute-start(f32[32,2560]{1,0:T(8,128)S(1)} %get-tuple-element.264), channel_id=1, source_target_pairs={{0,8},{8,16},{16,24},{24,0},{1,9},{9,17},{17,25},{25,1},{2,10},{10... | collective-permute-start | bytes 983048 | tf_op jit(solution)/shard_map/ppermute | solution.py:712
  112.8 15.1 %collective-permute-start.28 = (f32[32,2560]{1,0:T(8,128)S(1)}, f32[32,2560]{1,0:T(8,128)S(1)}, u32[]{:S(2)}, u32[]{:S(2)}) collective-permute-start(f32[32,2560]{1,0:T(8,128)S(1)} %get-tuple-element.265), channel_id=1, source_target_pairs={{0,16},{8,24},{16,0},{24,8},{1,17},{9,25},{17,1},{25,9},{2,18},{10... | collective-permute-start | bytes 983048 | tf_op jit(solution)/shard_map/ppermute | solution.py:712
  114.4 13.6 %collective-permute-start.29 = (f32[32,2560]{1,0:T(8,128)S(1)}, f32[32,2560]{1,0:T(8,128)S(1)}, u32[]{:S(2)}, u32[]{:S(2)}) collective-permute-start(f32[32,2560]{1,0:T(8,128)S(1)} %get-tuple-element.266), channel_id=1, source_target_pairs={{0,24},{8,0},{16,8},{24,16},{1,25},{9,1},{17,9},{25,17},{2,26},{10... | collective-permute-start | bytes 983048 | tf_op jit(solution)/shard_map/ppermute | solution.py:712
  120.6 11.8 %collective-permute-start.32 = (f32[128,512]{1,0:T(8,128)S(1)}, f32[128,512]{1,0:T(8,128)S(1)}, u32[]{:S(2)}, u32[]{:S(2)}) collective-permute-start(f32[128,512]{1,0:T(8,128)S(1)} %get-tuple-element.260.refs_14_), channel_id=1, source_target_pairs={{2,0},{3,1},{10,8},{11,9},{18,16},{19,17},{26,24},{27,25}} | collective-permute-start | bytes 786440 | tf_op jit(solution)/shard_map/ppermute | solution.py:646
  126.6 19.4 %collective-permute-start.36 = (f32[128,512]{1,0:T(8,128)S(1)}, f32[128,512]{1,0:T(8,128)S(1)}, u32[]{:S(2)}, u32[]{:S(2)}) collective-permute-start(f32[128,512]{1,0:T(8,128)S(1)} %get-tuple-element.271.refs_4_), channel_id=1, source_target_pairs={{2,0},{3,1},{10,8},{11,9},{18,16},{19,17},{26,24},{27,25}} | collective-permute-start | bytes 786440 | tf_op jit(solution)/shard_map/ppermute | solution.py:646
  151.4 13.5 %collective-permute-start.41 = (f32[32,2560]{1,0:T(8,128)S(1)}, f32[32,2560]{1,0:T(8,128)S(1)}, u32[]{:S(2)}, u32[]{:S(2)}) collective-permute-start(f32[32,2560]{1,0:T(8,128)S(1)} %shard_map.210.refs_6_), channel_id=1, source_target_pairs={{0,16},{8,24},{16,0},{24,8},{1,17},{9,25},{17,1},{25,9},{2,18},{10... | collective-permute-start | bytes 983048 | tf_op jit(solution)/shard_map/ppermute | solution.py:747
  (41 other events, 340.0 us)
